TPU v7x, 32 devices: a whole 2x2x4 slice. The times are simulated.
32 devices in a mesh: owner: 4 (over x, core), server: 8 (over z, y).
Axes of the slice: x: 2, y: 2, z: 4, core: 2. Of those that a mesh axis runs over, the one named last changes fastest.
Arguments:
- queries: bfloat16 [8192, 1024], P(('owner', 'server')), may hold values from -8 to 8
- key_vectors: bfloat16 [8192, 128], P(('owner', 'server')), may hold values from -8 to 8
- value_vectors: bfloat16 [8192, 128], P(('owner', 'server')), may hold values from -6 to 6
- out_grad: bfloat16 [8192, 1024], P(('owner', 'server')), may hold values from -6 to 6
- segments: int32 [8192], replicated, may hold values from 0 to 7, never falling along the last dimension, each value on 1 to 2048 neighbouring positions
- phase_label: int32 [32], P(('owner', 'server')), may hold values 0 or 1
Outputs:
- attn_out: bfloat16 [8192, 1024], P(('owner', 'server'))
- grad_query: bfloat16 [8192, 1024], P(('owner', 'server'))
- grad_key: float32 [8192, 128], P(('owner', 'server'))
- grad_value: float32 [8192, 128], P(('owner', 'server'))
All inputs are finite; a program needn't handle non-finite values. No bound on the sum of `phase_label` on one device may be relied on, other than what follows from the above.
Results may differ from a plain program's by a relative error of at most 0.012.
The roundings to bfloat16 on the way count: a program that leaves them out, or rounds other values in their place, can miss the bound.
Values may be sent and summed in bfloat16 or wider, within the bound.
No kernel may reach another device: no remote copies, remote signals or barrier semaphores. Data moves between devices by JAX's collectives and lax.ppermute only.
A program may use at most 128 MiB of HBM per device.

v0:
```python
import jax
import jax.numpy as jnp
from jax import lax
from jax.sharding import PartitionSpec as P

REACH = 8


def from_behind(block, axis, distance):
    devices = range(lax.axis_size(axis))
    route = [(i - distance, i) for i in devices if i - distance in devices]
    return lax.ppermute(block, axis, route)


def head_forward(query_head, key_window, value_window, allowed, score_scale):
    score = jnp.dot(query_head, key_window.T, preferred_element_type=jnp.float32) * score_scale
    score = jnp.where(allowed, score, -1e30)
    row_top = jnp.max(score, axis=1, keepdims=True)
    expos = jnp.exp(score - row_top)
    row_total = jnp.sum(expos, axis=1, keepdims=True)
    weights = expos.astype(jnp.bfloat16)
    head_out = jnp.dot(weights, value_window, preferred_element_type=jnp.float32) / row_total
    return (expos, row_total, head_out.astype(jnp.bfloat16))


def on_device(queries, key_vectors, value_vectors, out_grad, segments, phase_label):
    tok_rows = key_vectors.shape[0]
    width = key_vectors.shape[1]
    heads = queries.shape[1] // width
    key_span = (REACH + 1) * tok_rows
    score_scale = width ** (-0.5)
    my_index = lax.axis_index(("owner", "server"))
    parts_key = []
    parts_value = []
    for distance in range(REACH, 0, -1):
        moved_key, moved_value = from_behind(
            (key_vectors, value_vectors), ("owner", "server"), distance
        )
        parts_key.append(moved_key)
        parts_value.append(moved_value)
    key_window = jnp.concatenate(parts_key + [key_vectors], axis=0)
    value_window = jnp.concatenate(parts_value + [value_vectors], axis=0)
    segs_padded = jnp.concatenate([jnp.full((REACH * tok_rows,), -1, jnp.int32), segments], axis=0)
    key_segs = lax.dynamic_slice_in_dim(segs_padded, my_index * tok_rows, key_span, 0)
    query_segs = lax.dynamic_slice_in_dim(segments, my_index * tok_rows, tok_rows, 0)
    causal = jnp.arange(key_span)[None, :] <= jnp.arange(tok_rows)[:, None] + REACH * tok_rows
    allowed = causal & (query_segs[:, None] == key_segs[None, :])
    is_pong = phase_label[0] == 1
    outputs = []
    query_grads = []
    key_grad = jnp.zeros((key_span, width), jnp.float32)
    value_grad = jnp.zeros((key_span, width), jnp.float32)
    for head_index in range(heads):
        query_head = queries[:, head_index * width : (head_index + 1) * width]
        grad_head = out_grad[:, head_index * width : (head_index + 1) * width]
        expos, row_total, out_rounded = head_forward(
            query_head, key_window, value_window, allowed, score_scale
        )
        outputs.append(out_rounded)

        def backward(operands):
            expos_in, total_in, out_in = operands
            row_delta = jnp.sum(
                grad_head.astype(jnp.float32) * out_in.astype(jnp.float32), axis=1, keepdims=True
            )
            probs_full = expos_in / total_in
            grad_prob = jnp.dot(grad_head, value_window.T, preferred_element_type=jnp.float32)
            grad_score = (probs_full * (grad_prob - row_delta) * score_scale).astype(jnp.bfloat16)
            query_part = jnp.dot(grad_score, key_window, preferred_element_type=jnp.float32)
            key_part = jnp.dot(grad_score.T, query_head, preferred_element_type=jnp.float32)
            value_part = jnp.dot(
                probs_full.astype(jnp.bfloat16).T, grad_head, preferred_element_type=jnp.float32
            )
            return (query_part, key_part, value_part)

        def forward_only(operands):
            return (
                jnp.zeros((tok_rows, width), jnp.float32),
                jnp.zeros((key_span, width), jnp.float32),
                jnp.zeros((key_span, width), jnp.float32),
            )

        query_part, key_part, value_part = lax.cond(
            is_pong, backward, forward_only, (expos, row_total, out_rounded)
        )
        query_grads.append(query_part)
        key_grad = key_grad + key_part
        value_grad = value_grad + value_part
    attn_out = jnp.concatenate(outputs, axis=1)
    grad_query = jnp.concatenate(query_grads, axis=1).astype(jnp.bfloat16)
    grad_key = key_grad[REACH * tok_rows :]
    grad_value = value_grad[REACH * tok_rows :]
    for distance in range(1, REACH + 1):
        lower = (REACH - distance) * tok_rows
        back_key, back_value = (
            from_behind(
                key_grad[lower : lower + tok_rows].astype(jnp.bfloat16),
                ("owner", "server"),
                -distance,
            ).astype(jnp.float32),
            from_behind(
                value_grad[lower : lower + tok_rows].astype(jnp.bfloat16),
                ("owner", "server"),
                -distance,
            ).astype(jnp.float32),
        )
        grad_key = grad_key + back_key
        grad_value = grad_value + back_value
    return (attn_out, grad_query, grad_key, grad_value)


def solution(mesh):
    in_specs = (
        P(("owner", "server"), None),
        P(("owner", "server"), None),
        P(("owner", "server"), None),
        P(("owner", "server"), None),
        P(),
        P(("owner", "server")),
    )
    out_specs = (
        P(("owner", "server"), None),
        P(("owner", "server"), None),
        P(("owner", "server"), None),
        P(("owner", "server"), None),
    )
    return jax.shard_map(
        on_device, mesh=mesh, in_specs=in_specs, out_specs=out_specs, check_vma=False
    )
```

profile of v0, /device:TPU:7, one launch (start us, length us, event | category | flops | bytes accessed | tf_op | source)
XLA Modules:
  0.0 254.8 jit_solution(16452324619211155611)
XLA Ops:
  0.6 3.2 %collective-permute-start.6 = (bf16[256,128]{1,0:T(8,128)(2,1)}, bf16[256,128]{1,0:T(8,128)(2,1)S(1)}, u32[]{:S(2)}, u32[]{:S(2)}) collective-permute-start(bf16[256,128]{1,0:T(8,128)(2,1)} %param.23), channel_id=1, source_target_pairs={{0,2},{1,3},{2,4},{3,5},{4,6},{5,7},{6,8},{7,9},{8,10},{9,11},{10,... | collective-permute-start | bytes 196616 | tf_op jit(solution)/shard_map/ppermute | solution.py:12
  3.8 4.2 %collective-permute-start.5 = (bf16[256,128]{1,0:T(8,128)(2,1)}, bf16[256,128]{1,0:T(8,128)(2,1)S(1)}, u32[]{:S(2)}, u32[]{:S(2)}) collective-permute-start(bf16[256,128]{1,0:T(8,128)(2,1)} %param.23), channel_id=1, source_target_pairs={{0,3},{1,4},{2,5},{3,6},{4,7},{5,8},{6,9},{7,10},{8,11},{9,12},{10... | collective-permute-start | bytes 196616 | tf_op jit(solution)/shard_map/ppermute | solution.py:12
  8.0 1.9 collective-permute-start.4
  9.9 1.9 collective-permute-start.3
  20.0 5.5 %collective-permute-done.1 = bf16[256,128]{1,0:T(8,128)(2,1)S(1)} collective-permute-done((bf16[256,128]{1,0:T(8,128)(2,1)}, bf16[256,128]{1,0:T(8,128)(2,1)S(1)}, u32[]{:S(2)}, u32[]{:S(2)}) %collective-permute-start.1) | collective-permute-done | bytes 65568 | tf_op jit(solution)/shard_map/ppermute | solution.py:12
  25.5 2.0 collective-permute-start.2
  27.6 5.0 %collective-permute-done.2 = bf16[256,128]{1,0:T(8,128)(2,1)S(1)} collective-permute-done((bf16[256,128]{1,0:T(8,128)(2,1)}, bf16[256,128]{1,0:T(8,128)(2,1)S(1)}, u32[]{:S(2)}, u32[]{:S(2)}) %collective-permute-start.2) | collective-permute-done | bytes 65568 | tf_op jit(solution)/shard_map/ppermute | solution.py:12
  32.6 2.2 collective-permute-start.7
  34.8 2.6 %collective-permute-start.14 = (bf16[256,128]{1,0:T(8,128)(2,1)}, bf16[256,128]{1,0:T(8,128)(2,1)S(1)}, u32[]{:S(2)}, u32[]{:S(2)}) collective-permute-start(bf16[256,128]{1,0:T(8,128)(2,1)} %param.24), channel_id=1, source_target_pairs={{0,2},{1,3},{2,4},{3,5},{4,6},{5,7},{6,8},{7,9},{8,10},{9,11},{10,... | collective-permute-start | bytes 196616 | tf_op jit(solution)/shard_map/ppermute | solution.py:12
  37.5 4.4 %collective-permute-start.13 = (bf16[256,128]{1,0:T(8,128)(2,1)}, bf16[256,128]{1,0:T(8,128)(2,1)S(1)}, u32[]{:S(2)}, u32[]{:S(2)}) collective-permute-start(bf16[256,128]{1,0:T(8,128)(2,1)} %param.24), channel_id=1, source_target_pairs={{0,3},{1,4},{2,5},{3,6},{4,7},{5,8},{6,9},{7,10},{8,11},{9,12},{10... | collective-permute-start | bytes 196616 | tf_op jit(solution)/shard_map/ppermute | solution.py:12
  41.9 1.9 collective-permute-start.12
  43.8 1.9 collective-permute-start.11
  56.1 7.5 %collective-permute-done.9 = bf16[256,128]{1,0:T(8,128)(2,1)S(1)} collective-permute-done((bf16[256,128]{1,0:T(8,128)(2,1)S(1)}, bf16[256,128]{1,0:T(8,128)(2,1)S(1)}, u32[]{:S(2)}, u32[]{:S(2)}) %collective-permute-start.9) | collective-permute-done | bytes 65568 | tf_op jit(solution)/shard_map/ppermute | solution.py:12
  65.6 6.9 %collective-permute-done.10 = bf16[256,128]{1,0:T(8,128)(2,1)S(1)} collective-permute-done((bf16[256,128]{1,0:T(8,128)(2,1)S(1)}, bf16[256,128]{1,0:T(8,128)(2,1)S(1)}, u32[]{:S(2)}, u32[]{:S(2)}) %collective-permute-start.10) | collective-permute-done | bytes 65568 | tf_op jit(solution)/shard_map/ppermute | solution.py:12
  72.5 2.4 collective-permute-start.15
  75.0 2.5 collective-permute-done.15
  90.1 2.0 copy.26
  110.9 4.3 %fusion.159 = (bf16[2304,128]{1,0:T(8,128)(2,1)S(1)}, f32[2304,128]{1,0:T(8,128)S(1)}) fusion(f32[2304,128]{1,0:T(8,128)} %get-tuple-element.235, f32[2304,128]{1,0:T(8,128)} %get-tuple-element.234, f32[2304,128]{1,0:T(8,128)} %get-tuple-element.233, f32[2304,128]{1,0:T(8,128)} %get-tuple-element.232, f32[2304,128]{1,0:T(8,128)} %get-tuple-element.231, ...), kind=kLoop, calls=%fused_computation.216 | loop fusion | flops 2359296 | bytes 11206656 | tf_op jit(solution)/shard_map/convert.8
  117.9 5.2 %collective-permute-start.16 = (bf16[256,128]{1,0:T(8,128)(2,1)S(1)}, bf16[256,128]{1,0:T(8,128)(2,1)S(1)}, u32[]{:S(2)}, u32[]{:S(2)}) collective-permute-start(bf16[256,128]{1,0:T(8,128)(2,1)S(1)} %get-tuple-element.332), channel_id=1, source_target_pairs={{1,0},{2,1},{3,2},{4,3},{5,4},{6,5},{7,6},{8,7},{9,8},{10,9},{11,1... | collective-permute-start | bytes 196616 | tf_op jit(solution)/shard_map/ppermute | solution.py:12
  123.2 89.6 %collective-permute-start.23 = (bf16[256,128]{1,0:T(8,128)(2,1)S(1)}, bf16[256,128]{1,0:T(8,128)(2,1)S(1)}, u32[]{:S(2)}, u32[]{:S(2)}) collective-permute-start(bf16[256,128]{1,0:T(8,128)(2,1)S(1)} %get-tuple-element.333), channel_id=1, source_target_pairs={{8,0},{9,1},{10,2},{11,3},{12,4},{13,5},{14,6},{15,7},{16,8},{17,9... | collective-permute-start | bytes 196616 | tf_op jit(solution)/shard_map/ppermute | solution.py:12
  214.0 2.6 %collective-permute-start.21 = (bf16[256,128]{1,0:T(8,128)(2,1)S(1)}, bf16[256,128]{1,0:T(8,128)(2,1)S(1)}, u32[]{:S(2)}, u32[]{:S(2)}) collective-permute-start(bf16[256,128]{1,0:T(8,128)(2,1)S(1)} %get-tuple-element.335), channel_id=1, source_target_pairs={{6,0},{7,1},{8,2},{9,3},{10,4},{11,5},{12,6},{13,7},{14,8},{15,9},... | collective-permute-start | bytes 196616 | tf_op jit(solution)/shard_map/ppermute | solution.py:12
  216.6 4.8 %collective-permute-start.20 = (bf16[256,128]{1,0:T(8,128)(2,1)S(1)}, bf16[256,128]{1,0:T(8,128)(2,1)S(1)}, u32[]{:S(2)}, u32[]{:S(2)}) collective-permute-start(bf16[256,128]{1,0:T(8,128)(2,1)S(1)} %get-tuple-element.336), channel_id=1, source_target_pairs={{5,0},{6,1},{7,2},{8,3},{9,4},{10,5},{11,6},{12,7},{13,8},{14,9},{... | collective-permute-start | bytes 196616 | tf_op jit(solution)/shard_map/ppermute | solution.py:12
  221.7 4.1 %collective-permute-start.19 = (bf16[256,128]{1,0:T(8,128)(2,1)S(1)}, bf16[256,128]{1,0:T(8,128)(2,1)S(1)}, u32[]{:S(2)}, u32[]{:S(2)}) collective-permute-start(bf16[256,128]{1,0:T(8,128)(2,1)S(1)} %get-tuple-element.337), channel_id=1, source_target_pairs={{4,0},{5,1},{6,2},{7,3},{8,4},{9,5},{10,6},{11,7},{12,8},{13,9},{1... | collective-permute-start | bytes 196616 | tf_op jit(solution)/shard_map/ppermute | solution.py:12
  225.9 2.8 %collective-permute-start.18 = (bf16[256,128]{1,0:T(8,128)(2,1)S(1)}, bf16[256,128]{1,0:T(8,128)(2,1)S(1)}, u32[]{:S(2)}, u32[]{:S(2)}) collective-permute-start(bf16[256,128]{1,0:T(8,128)(2,1)S(1)} %get-tuple-element.338), channel_id=1, source_target_pairs={{3,0},{4,1},{5,2},{6,3},{7,4},{8,5},{9,6},{10,7},{11,8},{12,9},{13... | collective-permute-start | bytes 196616 | tf_op jit(solution)/shard_map/ppermute | solution.py:12
  228.7 3.1 %collective-permute-start.17 = (bf16[256,128]{1,0:T(8,128)(2,1)S(1)}, bf16[256,128]{1,0:T(8,128)(2,1)S(1)}, u32[]{:S(2)}, u32[]{:S(2)}) collective-permute-start(bf16[256,128]{1,0:T(8,128)(2,1)S(1)} %get-tuple-element.339), channel_id=1, source_target_pairs={{2,0},{3,1},{4,2},{5,3},{6,4},{7,5},{8,6},{9,7},{10,8},{11,9},{12,... | collective-permute-start | bytes 196616 | tf_op jit(solution)/shard_map/ppermute | solution.py:12
  231.8 3.1 %collective-permute-start.24 = (bf16[256,128]{1,0:T(8,128)(2,1)S(1)}, bf16[256,128]{1,0:T(8,128)(2,1)S(1)}, u32[]{:S(2)}, u32[]{:S(2)}) collective-permute-start(bf16[256,128]{1,0:T(8,128)(2,1)S(1)} %get-tuple-element.324), channel_id=1, source_target_pairs={{1,0},{2,1},{3,2},{4,3},{5,4},{6,5},{7,6},{8,7},{9,8},{10,9},{11,1... | collective-permute-start | bytes 196616 | tf_op jit(solution)/shard_map/ppermute | solution.py:12
  236.2 2.3 collective-permute-start.30
  240.5 3.4 %collective-permute-start.28 = (bf16[256,128]{1,0:T(8,128)(2,1)S(1)}, bf16[256,128]{1,0:T(8,128)(2,1)S(1)}, u32[]{:S(2)}, u32[]{:S(2)}) collective-permute-start(bf16[256,128]{1,0:T(8,128)(2,1)S(1)} %get-tuple-element.328), channel_id=1, source_target_pairs={{5,0},{6,1},{7,2},{8,3},{9,4},{10,5},{11,6},{12,7},{13,8},{14,9},{... | collective-permute-start | bytes 196616 | tf_op jit(solution)/shard_map/ppermute | solution.py:12
  243.9 1.9 collective-permute-start.27
  245.8 2.8 %collective-permute-start.26 = (bf16[256,128]{1,0:T(8,128)(2,1)S(1)}, bf16[256,128]{1,0:T(8,128)(2,1)S(1)}, u32[]{:S(2)}, u32[]{:S(2)}) collective-permute-start(bf16[256,128]{1,0:T(8,128)(2,1)S(1)} %get-tuple-element.330), channel_id=1, source_target_pairs={{3,0},{4,1},{5,2},{6,3},{7,4},{8,5},{9,6},{10,7},{11,8},{12,9},{13... | collective-permute-start | bytes 196616 | tf_op jit(solution)/shard_map/ppermute | solution.py:12
  248.7 2.5 collective-permute-start.25
  251.9 2.1 collective-permute-done.26
  (213 shorter events, 69.4 us)
Async XLA Ops:
  0.6 43.2 %collective-permute-start.6 = (bf16[256,128]{1,0:T(8,128)(2,1)}, bf16[256,128]{1,0:T(8,128)(2,1)S(1)}, u32[]{:S(2)}, u32[]{:S(2)}) collective-permute-start(bf16[256,128]{1,0:T(8,128)(2,1)} %param.23), channel_id=1, source_target_pairs={{0,2},{1,3},{2,4},{3,5},{4,6},{5,7},{6,8},{7,9},{8,10},{9,11},{10,... | collective-permute-start | bytes 196616 | tf_op jit(solution)/shard_map/ppermute | solution.py:12
  3.8 38.0 %collective-permute-start.5 = (bf16[256,128]{1,0:T(8,128)(2,1)}, bf16[256,128]{1,0:T(8,128)(2,1)S(1)}, u32[]{:S(2)}, u32[]{:S(2)}) collective-permute-start(bf16[256,128]{1,0:T(8,128)(2,1)} %param.23), channel_id=1, source_target_pairs={{0,3},{1,4},{2,5},{3,6},{4,7},{5,8},{6,9},{7,10},{8,11},{9,12},{10... | collective-permute-start | bytes 196616 | tf_op jit(solution)/shard_map/ppermute | solution.py:12
  8.0 29.4 %collective-permute-start.4 = (bf16[256,128]{1,0:T(8,128)(2,1)}, bf16[256,128]{1,0:T(8,128)(2,1)S(1)}, u32[]{:S(2)}, u32[]{:S(2)}) collective-permute-start(bf16[256,128]{1,0:T(8,128)(2,1)} %param.23), channel_id=1, source_target_pairs={{0,4},{1,5},{2,6},{3,7},{4,8},{5,9},{6,10},{7,11},{8,12},{9,13},{1... | collective-permute-start | bytes 196616 | tf_op jit(solution)/shard_map/ppermute | solution.py:12
  9.9 24.8 %collective-permute-start.3 = (bf16[256,128]{1,0:T(8,128)(2,1)}, bf16[256,128]{1,0:T(8,128)(2,1)S(1)}, u32[]{:S(2)}, u32[]{:S(2)}) collective-permute-start(bf16[256,128]{1,0:T(8,128)(2,1)} %param.23), channel_id=1, source_target_pairs={{0,5},{1,6},{2,7},{3,8},{4,9},{5,10},{6,11},{7,12},{8,13},{9,14},{... | collective-permute-start | bytes 196616 | tf_op jit(solution)/shard_map/ppermute | solution.py:12
  11.9 6.8 %collective-permute-start = (bf16[256,128]{1,0:T(8,128)(2,1)}, bf16[256,128]{1,0:T(8,128)(2,1)S(1)}, u32[]{:S(2)}, u32[]{:S(2)}) collective-permute-start(bf16[256,128]{1,0:T(8,128)(2,1)} %param.23), channel_id=1, source_target_pairs={{0,8},{1,9},{2,10},{3,11},{4,12},{5,13},{6,14},{7,15},{8,16},{9,17... | collective-permute-start | bytes 196616 | tf_op jit(solution)/shard_map/ppermute | solution.py:12
  18.7 6.8 %collective-permute-start.1 = (bf16[256,128]{1,0:T(8,128)(2,1)}, bf16[256,128]{1,0:T(8,128)(2,1)S(1)}, u32[]{:S(2)}, u32[]{:S(2)}) collective-permute-start(bf16[256,128]{1,0:T(8,128)(2,1)} %param.23), channel_id=1, source_target_pairs={{0,7},{1,8},{2,9},{3,10},{4,11},{5,12},{6,13},{7,14},{8,15},{9,16}... | collective-permute-start | bytes 196616 | tf_op jit(solution)/shard_map/ppermute | solution.py:12
  25.5 7.0 %collective-permute-start.2 = (bf16[256,128]{1,0:T(8,128)(2,1)}, bf16[256,128]{1,0:T(8,128)(2,1)S(1)}, u32[]{:S(2)}, u32[]{:S(2)}) collective-permute-start(bf16[256,128]{1,0:T(8,128)(2,1)} %param.23), channel_id=1, source_target_pairs={{0,6},{1,7},{2,8},{3,9},{4,10},{5,11},{6,12},{7,13},{8,14},{9,15},... | collective-permute-start | bytes 196616 | tf_op jit(solution)/shard_map/ppermute | solution.py:12
  32.6 13.2 %collective-permute-start.7 = (bf16[256,128]{1,0:T(8,128)(2,1)}, bf16[256,128]{1,0:T(8,128)(2,1)S(1)}, u32[]{:S(2)}, u32[]{:S(2)}) collective-permute-start(bf16[256,128]{1,0:T(8,128)(2,1)} %param.23), channel_id=1, source_target_pairs={{0,1},{1,2},{2,3},{3,4},{4,5},{5,6},{6,7},{7,8},{8,9},{9,10},{10,1... | collective-permute-start | bytes 196616 | tf_op jit(solution)/shard_map/ppermute | solution.py:12
  34.8 40.2 %collective-permute-start.14 = (bf16[256,128]{1,0:T(8,128)(2,1)}, bf16[256,128]{1,0:T(8,128)(2,1)S(1)}, u32[]{:S(2)}, u32[]{:S(2)}) collective-permute-start(bf16[256,128]{1,0:T(8,128)(2,1)} %param.24), channel_id=1, source_target_pairs={{0,2},{1,3},{2,4},{3,5},{4,6},{5,7},{6,8},{7,9},{8,10},{9,11},{10,... | collective-permute-start | bytes 196616 | tf_op jit(solution)/shard_map/ppermute | solution.py:12
  37.5 37.5 %collective-permute-start.13 = (bf16[256,128]{1,0:T(8,128)(2,1)}, bf16[256,128]{1,0:T(8,128)(2,1)S(1)}, u32[]{:S(2)}, u32[]{:S(2)}) collective-permute-start(bf16[256,128]{1,0:T(8,128)(2,1)} %param.24), channel_id=1, source_target_pairs={{0,3},{1,4},{2,5},{3,6},{4,7},{5,8},{6,9},{7,10},{8,11},{9,12},{10... | collective-permute-start | bytes 196616 | tf_op jit(solution)/shard_map/ppermute | solution.py:12
  41.9 33.1 %collective-permute-start.12 = (bf16[256,128]{1,0:T(8,128)(2,1)}, bf16[256,128]{1,0:T(8,128)(2,1)S(1)}, u32[]{:S(2)}, u32[]{:S(2)}) collective-permute-start(bf16[256,128]{1,0:T(8,128)(2,1)} %param.24), channel_id=1, source_target_pairs={{0,4},{1,5},{2,6},{3,7},{4,8},{5,9},{6,10},{7,11},{8,12},{9,13},{1... | collective-permute-start | bytes 196616 | tf_op jit(solution)/shard_map/ppermute | solution.py:12
  43.8 31.1 %collective-permute-start.11 = (bf16[256,128]{1,0:T(8,128)(2,1)}, bf16[256,128]{1,0:T(8,128)(2,1)S(1)}, u32[]{:S(2)}, u32[]{:S(2)}) collective-permute-start(bf16[256,128]{1,0:T(8,128)(2,1)} %param.24), channel_id=1, source_target_pairs={{0,5},{1,6},{2,7},{3,8},{4,9},{5,10},{6,11},{7,12},{8,13},{9,14},{... | collective-permute-start | bytes 196616 | tf_op jit(solution)/shard_map/ppermute | solution.py:12
  45.8 8.9 %collective-permute-start.8 = (bf16[256,128]{1,0:T(8,128)(2,1)}, bf16[256,128]{1,0:T(8,128)(2,1)S(1)}, u32[]{:S(2)}, u32[]{:S(2)}) collective-permute-start(bf16[256,128]{1,0:T(8,128)(2,1)} %param.24), channel_id=1, source_target_pairs={{0,8},{1,9},{2,10},{3,11},{4,12},{5,13},{6,14},{7,15},{8,16},{9,17... | collective-permute-start | bytes 196616 | tf_op jit(solution)/shard_map/ppermute | solution.py:12
  54.8 8.8 %collective-permute-start.9 = (bf16[256,128]{1,0:T(8,128)(2,1)S(1)}, bf16[256,128]{1,0:T(8,128)(2,1)S(1)}, u32[]{:S(2)}, u32[]{:S(2)}) collective-permute-start(bf16[256,128]{1,0:T(8,128)(2,1)S(1)} %copy-done.56), channel_id=1, source_target_pairs={{0,7},{1,8},{2,9},{3,10},{4,11},{5,12},{6,13},{7,14},{8,15},{9,16}... | collective-permute-start | bytes 196616 | tf_op jit(solution)/shard_map/ppermute | solution.py:12
  63.7 8.8 %collective-permute-start.10 = (bf16[256,128]{1,0:T(8,128)(2,1)S(1)}, bf16[256,128]{1,0:T(8,128)(2,1)S(1)}, u32[]{:S(2)}, u32[]{:S(2)}) collective-permute-start(bf16[256,128]{1,0:T(8,128)(2,1)S(1)} %copy-done.56), channel_id=1, source_target_pairs={{0,6},{1,7},{2,8},{3,9},{4,10},{5,11},{6,12},{7,13},{8,14},{9,15},... | collective-permute-start | bytes 196616 | tf_op jit(solution)/shard_map/ppermute | solution.py:12
  72.5 5.0 %collective-permute-start.15 = (bf16[256,128]{1,0:T(8,128)(2,1)S(1)}, bf16[256,128]{1,0:T(8,128)(2,1)S(1)}, u32[]{:S(2)}, u32[]{:S(2)}) collective-permute-start(bf16[256,128]{1,0:T(8,128)(2,1)S(1)} %copy-done.56), channel_id=1, source_target_pairs={{0,1},{1,2},{2,3},{3,4},{4,5},{5,6},{6,7},{7,8},{8,9},{9,10},{10,1... | collective-permute-start | bytes 196616 | tf_op jit(solution)/shard_map/ppermute | solution.py:12
  117.9 103.7 %collective-permute-start.16 = (bf16[256,128]{1,0:T(8,128)(2,1)S(1)}, bf16[256,128]{1,0:T(8,128)(2,1)S(1)}, u32[]{:S(2)}, u32[]{:S(2)}) collective-permute-start(bf16[256,128]{1,0:T(8,128)(2,1)S(1)} %get-tuple-element.332), channel_id=1, source_target_pairs={{1,0},{2,1},{3,2},{4,3},{5,4},{6,5},{7,6},{8,7},{9,8},{10,9},{11,1... | collective-permute-start | bytes 196616 | tf_op jit(solution)/shard_map/ppermute | solution.py:12
  123.2 102.7 %collective-permute-start.23 = (bf16[256,128]{1,0:T(8,128)(2,1)S(1)}, bf16[256,128]{1,0:T(8,128)(2,1)S(1)}, u32[]{:S(2)}, u32[]{:S(2)}) collective-permute-start(bf16[256,128]{1,0:T(8,128)(2,1)S(1)} %get-tuple-element.333), channel_id=1, source_target_pairs={{8,0},{9,1},{10,2},{11,3},{12,4},{13,5},{14,6},{15,7},{16,8},{17,9... | collective-permute-start | bytes 196616 | tf_op jit(solution)/shard_map/ppermute | solution.py:12
  212.7 15.9 %collective-permute-start.22 = (bf16[256,128]{1,0:T(8,128)(2,1)S(1)}, bf16[256,128]{1,0:T(8,128)(2,1)S(1)}, u32[]{:S(2)}, u32[]{:S(2)}) collective-permute-start(bf16[256,128]{1,0:T(8,128)(2,1)S(1)} %get-tuple-element.334), channel_id=1, source_target_pairs={{7,0},{8,1},{9,2},{10,3},{11,4},{12,5},{13,6},{14,7},{15,8},{16,9}... | collective-permute-start | bytes 196616 | tf_op jit(solution)/shard_map/ppermute | solution.py:12
  214.0 17.8 %collective-permute-start.21 = (bf16[256,128]{1,0:T(8,128)(2,1)S(1)}, bf16[256,128]{1,0:T(8,128)(2,1)S(1)}, u32[]{:S(2)}, u32[]{:S(2)}) collective-permute-start(bf16[256,128]{1,0:T(8,128)(2,1)S(1)} %get-tuple-element.335), channel_id=1, source_target_pairs={{6,0},{7,1},{8,2},{9,3},{10,4},{11,5},{12,6},{13,7},{14,8},{15,9},... | collective-permute-start | bytes 196616 | tf_op jit(solution)/shard_map/ppermute | solution.py:12
  216.6 18.3 %collective-permute-start.20 = (bf16[256,128]{1,0:T(8,128)(2,1)S(1)}, bf16[256,128]{1,0:T(8,128)(2,1)S(1)}, u32[]{:S(2)}, u32[]{:S(2)}) collective-permute-start(bf16[256,128]{1,0:T(8,128)(2,1)S(1)} %get-tuple-element.336), channel_id=1, source_target_pairs={{5,0},{6,1},{7,2},{8,3},{9,4},{10,5},{11,6},{12,7},{13,8},{14,9},{... | collective-permute-start | bytes 196616 | tf_op jit(solution)/shard_map/ppermute | solution.py:12
  221.7 14.6 %collective-permute-start.19 = (bf16[256,128]{1,0:T(8,128)(2,1)S(1)}, bf16[256,128]{1,0:T(8,128)(2,1)S(1)}, u32[]{:S(2)}, u32[]{:S(2)}) collective-permute-start(bf16[256,128]{1,0:T(8,128)(2,1)S(1)} %get-tuple-element.337), channel_id=1, source_target_pairs={{4,0},{5,1},{6,2},{7,3},{8,4},{9,5},{10,6},{11,7},{12,8},{13,9},{1... | collective-permute-start | bytes 196616 | tf_op jit(solution)/shard_map/ppermute | solution.py:12
  225.9 12.7 %collective-permute-start.18 = (bf16[256,128]{1,0:T(8,128)(2,1)S(1)}, bf16[256,128]{1,0:T(8,128)(2,1)S(1)}, u32[]{:S(2)}, u32[]{:S(2)}) collective-permute-start(bf16[256,128]{1,0:T(8,128)(2,1)S(1)} %get-tuple-element.338), channel_id=1, source_target_pairs={{3,0},{4,1},{5,2},{6,3},{7,4},{8,5},{9,6},{10,7},{11,8},{12,9},{13... | collective-permute-start | bytes 196616 | tf_op jit(solution)/shard_map/ppermute | solution.py:12
  228.7 11.8 %collective-permute-start.17 = (bf16[256,128]{1,0:T(8,128)(2,1)S(1)}, bf16[256,128]{1,0:T(8,128)(2,1)S(1)}, u32[]{:S(2)}, u32[]{:S(2)}) collective-permute-start(bf16[256,128]{1,0:T(8,128)(2,1)S(1)} %get-tuple-element.339), channel_id=1, source_target_pairs={{2,0},{3,1},{4,2},{5,3},{6,4},{7,5},{8,6},{9,7},{10,8},{11,9},{12,... | collective-permute-start | bytes 196616 | tf_op jit(solution)/shard_map/ppermute | solution.py:12
  231.8 12.1 %collective-permute-start.24 = (bf16[256,128]{1,0:T(8,128)(2,1)S(1)}, bf16[256,128]{1,0:T(8,128)(2,1)S(1)}, u32[]{:S(2)}, u32[]{:S(2)}) collective-permute-start(bf16[256,128]{1,0:T(8,128)(2,1)S(1)} %get-tuple-element.324), channel_id=1, source_target_pairs={{1,0},{2,1},{3,2},{4,3},{5,4},{6,5},{7,6},{8,7},{9,8},{10,9},{11,1... | collective-permute-start | bytes 196616 | tf_op jit(solution)/shard_map/ppermute | solution.py:12
  234.9 10.9 %collective-permute-start.31 = (bf16[256,128]{1,0:T(8,128)(2,1)S(1)}, bf16[256,128]{1,0:T(8,128)(2,1)S(1)}, u32[]{:S(2)}, u32[]{:S(2)}) collective-permute-start(bf16[256,128]{1,0:T(8,128)(2,1)S(1)} %get-tuple-element.325), channel_id=1, source_target_pairs={{8,0},{9,1},{10,2},{11,3},{12,4},{13,5},{14,6},{15,7},{16,8},{17,9... | collective-permute-start | bytes 196616 | tf_op jit(solution)/shard_map/ppermute | solution.py:12
  236.2 12.4 %collective-permute-start.30 = (bf16[256,128]{1,0:T(8,128)(2,1)S(1)}, bf16[256,128]{1,0:T(8,128)(2,1)S(1)}, u32[]{:S(2)}, u32[]{:S(2)}) collective-permute-start(bf16[256,128]{1,0:T(8,128)(2,1)S(1)} %get-tuple-element.326), channel_id=1, source_target_pairs={{7,0},{8,1},{9,2},{10,3},{11,4},{12,5},{13,6},{14,7},{15,8},{16,9}... | collective-permute-start | bytes 196616 | tf_op jit(solution)/shard_map/ppermute | solution.py:12
  238.6 13.3 %collective-permute-start.29 = (bf16[256,128]{1,0:T(8,128)(2,1)S(1)}, bf16[256,128]{1,0:T(8,128)(2,1)S(1)}, u32[]{:S(2)}, u32[]{:S(2)}) collective-permute-start(bf16[256,128]{1,0:T(8,128)(2,1)S(1)} %get-tuple-element.327), channel_id=1, source_target_pairs={{6,0},{7,1},{8,2},{9,3},{10,4},{11,5},{12,6},{13,7},{14,8},{15,9},... | collective-permute-start | bytes 196616 | tf_op jit(solution)/shard_map/ppermute | solution.py:12
  240.5 11.4 %collective-permute-start.28 = (bf16[256,128]{1,0:T(8,128)(2,1)S(1)}, bf16[256,128]{1,0:T(8,128)(2,1)S(1)}, u32[]{:S(2)}, u32[]{:S(2)}) collective-permute-start(bf16[256,128]{1,0:T(8,128)(2,1)S(1)} %get-tuple-element.328), channel_id=1, source_target_pairs={{5,0},{6,1},{7,2},{8,3},{9,4},{10,5},{11,6},{12,7},{13,8},{14,9},{... | collective-permute-start | bytes 196616 | tf_op jit(solution)/shard_map/ppermute | solution.py:12
  243.9 8.0 %collective-permute-start.27 = (bf16[256,128]{1,0:T(8,128)(2,1)S(1)}, bf16[256,128]{1,0:T(8,128)(2,1)S(1)}, u32[]{:S(2)}, u32[]{:S(2)}) collective-permute-start(bf16[256,128]{1,0:T(8,128)(2,1)S(1)} %get-tuple-element.329), channel_id=1, source_target_pairs={{4,0},{5,1},{6,2},{7,3},{8,4},{9,5},{10,6},{11,7},{12,8},{13,9},{1... | collective-permute-start | bytes 196616 | tf_op jit(solution)/shard_map/ppermute | solution.py:12
  245.8 8.2 %collective-permute-start.26 = (bf16[256,128]{1,0:T(8,128)(2,1)S(1)}, bf16[256,128]{1,0:T(8,128)(2,1)S(1)}, u32[]{:S(2)}, u32[]{:S(2)}) collective-permute-start(bf16[256,128]{1,0:T(8,128)(2,1)S(1)} %get-tuple-element.330), channel_id=1, source_target_pairs={{3,0},{4,1},{5,2},{6,3},{7,4},{8,5},{9,6},{10,7},{11,8},{12,9},{13... | collective-permute-start | bytes 196616 | tf_op jit(solution)/shard_map/ppermute | solution.py:12
  248.7 5.4 %collective-permute-start.25 = (bf16[256,128]{1,0:T(8,128)(2,1)S(1)}, bf16[256,128]{1,0:T(8,128)(2,1)S(1)}, u32[]{:S(2)}, u32[]{:S(2)}) collective-permute-start(bf16[256,128]{1,0:T(8,128)(2,1)S(1)} %get-tuple-element.331), channel_id=1, source_target_pairs={{2,0},{3,1},{4,2},{5,3},{6,4},{7,5},{8,6},{9,7},{10,8},{11,9},{12,... | collective-permute-start | bytes 196616 | tf_op jit(solution)/shard_map/ppermute | solution.py:12
  (46 other events, 961.7 us)
where the time goes:
time: 257 us; the launch traced here: 255 us
  starting transfers between devices  168 us (65%)
  waiting for transfers between devices  31.1 us (12%)
  local copies, waits for them, and re-layouts  27.1 us (11%)
  matrix products  16.5 us (6%)
  other arithmetic  8.79 us (3%)
    ppermute x32, starting transfers between devices, from_behind(): return lax.ppermute(block, axis, route)  168 us
    ppermute x32, waiting for transfers between devices, from_behind(): return lax.ppermute(block, axis, route)  31.1 us
    unnamed x116, local copies, waits for them, and re-layouts  13.1 us
    dot_general x8, matrix products, head_forward(): jnp.dot(weights, value_window, preferred_element_type=jnp.float32)  9.86 us
    another operation x24, local copies, waits for them, and re-layouts  9.6 us
    dot_general x8, matrix products, head_forward(): jnp.dot(query_head, key_window.T, preferred_element_type=jnp.float32)  6.59 us
  transfers between devices with their start and end apart: 32, of which 7 were waited for; matrix products, arithmetic and copies ran while one was open for 5% of the time, Pallas kernels for 0%

commit v1 on v0

v1 whole, which is shorter than its diff:
```python
import functools
import math

import jax
import jax.numpy as jnp
from jax import lax
from jax.experimental import pallas as pl
from jax.experimental.pallas import tpu as pltpu
from jax.sharding import PartitionSpec as P

REACH = 8
NEG = -1e30
AXES = ("owner", "server")
NT = (((1,), (1,)), ((), ()))
NN = (((1,), (0,)), ((), ()))
BF = jnp.bfloat16
F32 = jnp.float32
VMEM = pl.BlockSpec(memory_space=pltpu.VMEM)
SMEM = pl.BlockSpec(memory_space=pltpu.SMEM)


def room(mib):
    return pltpu.CompilerParams(vmem_limit_bytes=mib << 20)


OWN = -1
NEAR = ((0, OWN), (4, 6, 2, 1))


def dot(a, b, dims=NN):
    return lax.dot_general(a, b, dims, preferred_element_type=F32)


def pack_pair(k_ref, v_ref, kv_ref, sems):
    width = k_ref.shape[1]
    copies = [
        pltpu.make_async_copy(src, kv_ref.at[:, pl.ds(i * width, width)], sems.at[i])
        for i, src in enumerate((k_ref, v_ref))
    ]
    for copy in copies:
        copy.start()
    for copy in copies:
        copy.wait()


def choose(place_ref, kv_ref, before_ref, *outs):
    for bit, out in zip((4, 2, 1), outs, strict=True):
        ahead = (place_ref[0] & bit) == 0

        @pl.when(ahead)
        def _():
            out[...] = kv_ref[...]

        @pl.when(jnp.logical_not(ahead))
        def _():
            out[...] = before_ref[...]


def document_starts(me_ref, seg_ref, start_ref, first_ref):
    lanes = seg_ref.shape[1]
    tok = start_ref.shape[1]
    base = pl.multiple_of(me_ref[0] * (tok // lanes), tok // lanes)
    row = jnp.concatenate([seg_ref[pl.ds(base + j, 1), :] for j in range(tok // lanes)], axis=1)
    grid = jnp.broadcast_to(row, (tok, tok))
    inside = jnp.sum((grid.T < grid).astype(jnp.int32), axis=0, keepdims=True)
    head = jnp.sum((seg_ref[...] < row[0, 0]).astype(jnp.int32)) - me_ref[0] * tok
    start_ref[...] = jnp.where(inside > 0, inside, head)
    first_ref[0] = head


def tile_views(ctx, place, bit):
    if bit == OWN:
        return 0
    back = ((place - (place ^ bit) + 2 * REACH - 1) & (REACH - 1)) + 1
    return -back * ctx.tok


class Sizes:
    def __init__(self, heads, tok, width):
        self.heads, self.tok, self.width = heads, tok, width
        self.rows = heads * tok
        self.scale = width**-0.5
        self.c = self.scale * math.log2(math.e)

    def lanes(self, h):
        return slice(h * self.tok, (h + 1) * self.tok)

    def cols(self, h):
        return slice(h * self.width, (h + 1) * self.width)


def stack_heads(z, src, dst):
    for h in range(z.heads):
        dst[z.lanes(h), :] = src[:, z.cols(h)]


def masked(z, s, start_ref, rel, own):
    rows = lax.broadcasted_iota(jnp.int32, (z.tok, z.tok), 0)
    ok = rows >= start_ref[0:1, :] - rel
    if own:
        ok = ok & (rows <= lax.broadcasted_iota(jnp.int32, (z.tok, z.tok), 1))
    return jnp.where(ok, s, NEG)


def backward_tile(z, tile, prob, qs, gs, delta, p_buf, d_buf, dq_acc, fresh):
    v = tile[:, z.width :]
    kt = tile[:, : z.width].T
    for h in range(z.heads):
        lanes = z.lanes(h)
        p = prob(h)
        dp = dot(v, gs[lanes, :], NT)
        d_buf[:, lanes] = (p * (dp - delta[0:1, lanes])).astype(BF)
        p_buf[:, lanes] = p.astype(BF)
    part = dot(kt, d_buf[...])
    dq_acc[...] = part if fresh else dq_acc[...] + part
    return dot(d_buf[...], qs[...]) * z.scale, dot(p_buf[...], gs[...])


def forward_kernel(z, order, fresh, early, *refs):
    refs = list(refs)
    place_ref, first_ref, pong, q_ref = refs[:4]
    g_ref = refs.pop(4) if early else None
    start_ref = refs[4]
    n = len(order)
    at = 5
    if not fresh:
        old_top, old_total, old_acc = refs[at : at + 3]
        at += 3
    kv_refs = refs[at : at + n]
    at += n
    if early:
        out_ref, top, delta, dq_acc = refs[at : at + 4]
        at += 4
        part_refs = refs[at : at + early]
        at += early
        total, acc, gs, d_buf = refs[at : at + 4]
        at += 4
    else:
        top, total, acc = refs[at : at + 3]
        at += 3
    qs, p_buf, tiles, s_buf = refs[at:]
    groups = z.tok // 8
    loop = n - 1 if fresh else n
    stack_heads(z, q_ref, qs)
    for i in range(n):
        tiles[i] = kv_refs[i][...]

    def scores(i, rel, own):
        k = tiles[i, :, : z.width]
        for h in range(z.heads):
            lanes = z.lanes(h)
            s = masked(z, dot(k, qs[lanes, :], NT) * z.c, start_ref, rel, own)
            s_buf[i, :, lanes] = s
            m = jnp.max(s.reshape(groups, 8, z.tok), axis=0)
            top[:, lanes] = m if own else jnp.maximum(top[:, lanes], m)

    def forward(i, own):
        vt = tiles[i, :, z.width :].T
        for h in range(z.heads):
            lanes = z.lanes(h)
            p = jnp.exp2(s_buf[i, :, lanes] - top[0:1, lanes])
            t = jnp.sum(p.reshape(groups, 8, z.tok), axis=0)
            p_buf[:, lanes] = p.astype(BF)
            total[:, lanes] = t if own else total[:, lanes] + t
        o = dot(vt, p_buf[...])
        acc[...] = o if own else acc[...] + o

    place = place_ref[0]
    rels = [tile_views(z, place, bit) for bit in order]

    def each_seen(visit):
        def step(i, carry):
            rel = rels[0]
            for j in range(1, loop):
                rel = jnp.where(i == j, rels[j], rel)

            @pl.when(rel + z.tok > first_ref[0])
            def _():
                visit(i, rel)

            return carry

        lax.fori_loop(0, loop, step, 0)

    if fresh:
        scores(n - 1, 0, True)
    else:
        top[...] = jnp.broadcast_to(old_top[0:1, :], top.shape)
    each_seen(lambda i, rel: scores(i, rel, False))
    top[0:1, :] = jnp.max(top[...], axis=0, keepdims=True)
    if fresh:
        forward(n - 1, True)
    else:
        alpha = jnp.exp2(old_top[0:1, :] - top[0:1, :])
        total[...] = old_total[...] * alpha
        acc[...] = old_acc[...] * alpha
    each_seen(lambda i, rel: forward(i, False))
    if not early:
        return

    for h in range(z.heads):
        lanes = z.lanes(h)
        sums = jnp.sum(total[:, lanes], axis=0, keepdims=True)
        o = (acc[:, lanes] / sums).T.astype(BF)
        out_ref[:, z.cols(h)] = o
        prod = g_ref[:, z.cols(h)].astype(F32) * o.astype(F32)
        delta[0:1, lanes] = jnp.sum(prod.T, axis=0, keepdims=True)
        top[0:1, lanes] = top[0:1, lanes] + jnp.log2(sums)

    dq_acc[...] = jnp.zeros_like(dq_acc)
    for part in part_refs:
        part[...] = jnp.zeros_like(part)

    @pl.when(pong[0] == 1)
    def _():
        stack_heads(z, g_ref, gs)
        for i in range(early):

            @pl.when(rels[i] + z.tok > first_ref[0])
            def _():
                def prob(h):
                    return jnp.exp2(s_buf[i, :, z.lanes(h)] - top[0:1, z.lanes(h)])

                dk, dv = backward_tile(z, kv_refs[i], prob, qs, gs, delta, p_buf, d_buf, dq_acc, False)
                part_refs[i][:, : z.width] = dk.astype(BF)
                part_refs[i][:, z.width :] = dv.astype(BF)


def backward_kernel(z, order, last, *refs):
    place_ref, first_ref, pong = refs[:3]
    q_ref, g_ref, start_ref, top, delta, dq_in = refs[3:9]
    n = len(order)
    kv_refs = refs[9 : 9 + n]
    out_ref = refs[9 + n]
    part_refs = refs[10 + n : 10 + 2 * n]
    qs, gs, p_buf, d_buf = refs[10 + 2 * n : 14 + 2 * n]
    dq_acc = refs[14 + 2 * n] if last else out_ref
    place = place_ref[0]

    @pl.when(pong[0] == 1)
    def _():
        stack_heads(z, q_ref, qs)
        stack_heads(z, g_ref, gs)
        dq_acc[...] = dq_in[...]
        for i, bit in enumerate(order):
            rel = tile_views(z, place, bit)
            seen = rel + z.tok > first_ref[0]

            @pl.when(seen)
            def _():
                def prob(h):
                    s = dot(kv_refs[i][:, : z.width], qs[z.lanes(h), :], NT) * z.c
                    s = masked(z, s, start_ref, rel, bit == OWN)
                    return jnp.exp2(s - top[0:1, z.lanes(h)])

                dk, dv = backward_tile(z, kv_refs[i], prob, qs, gs, delta, p_buf, d_buf, dq_acc, False)
                part_refs[i][:, : z.width] = dk.astype(part_refs[i].dtype)
                part_refs[i][:, z.width :] = dv.astype(part_refs[i].dtype)

            @pl.when(jnp.logical_not(seen))
            def _():
                part_refs[i][...] = jnp.zeros_like(part_refs[i])

        if last:
            for h in range(z.heads):
                out_ref[:, z.cols(h)] = (dq_acc[:, z.lanes(h)] * z.scale).T.astype(BF)

    @pl.when(pong[0] != 1)
    def _():
        out_ref[...] = jnp.zeros_like(out_ref)
        for part in part_refs:
            part[...] = jnp.zeros_like(part)


def cost(z, tiles, products):
    pairs = z.rows * tiles * z.tok
    return pl.CostEstimate(
        flops=2 * products * pairs * z.width, bytes_accessed=6 << 20, transcendentals=pairs
    )


def run_forward(z, scalars, queries, out_grad, start, state, tiles, order, early):
    n = len(order)
    shape = jax.ShapeDtypeStruct
    stats, wide = shape((8, z.rows), F32), shape((z.width, z.rows), F32)
    scratch = [
        pltpu.VMEM((z.rows, z.width), BF),
        pltpu.VMEM((z.tok, z.rows), BF),
        pltpu.VMEM((n, z.tok, 2 * z.width), BF),
        pltpu.VMEM((n, z.tok, z.rows), F32),
    ]
    if early:
        outs = [shape(queries.shape, BF), stats, stats, wide] + [shape((z.tok, 2 * z.width), BF)] * early
        scratch = [
            pltpu.VMEM((8, z.rows), F32),
            pltpu.VMEM((z.width, z.rows), F32),
            pltpu.VMEM((z.rows, z.width), BF),
            pltpu.VMEM((z.tok, z.rows), BF),
        ] + scratch
    else:
        outs = [stats, stats, wide]
    args = [queries, out_grad, start] if early else [queries, start]
    args += list(state) + list(tiles)
    return pl.pallas_call(
        functools.partial(forward_kernel, z, order, not state, early),
        out_shape=outs,
        in_specs=[SMEM] * 3 + [VMEM] * len(args),
        out_specs=[VMEM] * len(outs),
        scratch_shapes=scratch,
        compiler_params=room(24 if early else 16),
        cost_estimate=cost(z, n, 4),
    )(*scalars, *args)


def run_backward(z, scalars, queries, out_grad, start, state, tiles, order, last):
    n = len(order)
    shape = jax.ShapeDtypeStruct
    dq = shape(queries.shape, BF) if last else shape((z.width, z.rows), F32)
    parts = [shape((z.tok, 2 * z.width), F32 if bit == OWN else BF) for bit in order]
    return pl.pallas_call(
        functools.partial(backward_kernel, z, order, last),
        out_shape=[dq] + parts,
        in_specs=[SMEM] * 3 + [VMEM] * (6 + n),
        out_specs=[VMEM] * (1 + n),
        scratch_shapes=[
            pltpu.VMEM((z.rows, z.width), BF),
            pltpu.VMEM((z.rows, z.width), BF),
            pltpu.VMEM((z.tok, z.rows), BF),
            pltpu.VMEM((z.tok, z.rows), BF),
        ]
        + ([pltpu.VMEM((z.width, z.rows), F32)] if last else []),
        compiler_params=room(10),
        cost_estimate=cost(z, n, 10),
    )(*scalars, queries, out_grad, start, *state, *tiles)


def on_device(queries, key_vectors, value_vectors, out_grad, segments, phase_label):
    tok, width = key_vectors.shape
    z = Sizes(queries.shape[1] // width, tok, width)
    devices = lax.axis_size(AXES)
    me = lax.axis_index(AXES).astype(jnp.int32)
    place = me & (REACH - 1)
    shape = jax.ShapeDtypeStruct
    block = shape((tok, 2 * width), BF)

    def swap(x, bit):
        return lax.ppermute(x, AXES, [(i, i ^ bit) for i in range(devices)])

    def shift(x, by):
        pairs = [(i, i + by) for i in range(devices) if 0 <= i + by < devices]
        return lax.ppermute(x, AXES, pairs)

    def give_back(x, bit):
        pairs = [(i, i ^ bit if i & bit else (i ^ bit) - REACH) for i in range(devices)]
        return lax.ppermute(x, AXES, [(i, j) for i, j in pairs if j >= 0])

    kv = pl.pallas_call(
        pack_pair,
        out_shape=block,
        in_specs=[pl.BlockSpec(memory_space=pltpu.HBM)] * 2,
        out_specs=VMEM,
        scratch_shapes=[pltpu.SemaphoreType.DMA((2,))],
        compiler_params=room(4),
    )(key_vectors, value_vectors)
    before = shift(kv, REACH)
    start, first = pl.pallas_call(
        document_starts,
        out_shape=[shape((1, tok), jnp.int32), shape((1,), jnp.int32)],
        in_specs=[SMEM, VMEM],
        out_specs=[VMEM, SMEM],
        compiler_params=room(4),
    )(me[None], segments.reshape(-1, 128))
    ahead = pl.pallas_call(
        choose, out_shape=[block] * 3, in_specs=[SMEM] + [VMEM] * 2, out_specs=[VMEM] * 3, compiler_params=room(4)
    )(place[None], kv, before)
    slot = {0: before, 4: swap(ahead[0], 4), 2: swap(ahead[1], 2)}
    slot[1] = swap(ahead[2], 1)
    slot[5] = swap(slot[4], 1)
    slot[6] = swap(slot[4], 2)
    slot[3] = swap(slot[2], 1)
    slot[7] = swap(slot[5], 2)

    scalars = (place[None], first, phase_label)
    slot[OWN] = kv
    state = ()
    for near in NEAR:
        state = run_forward(z, scalars, queries, None, start, state, [slot[b] for b in near], near, 0)
    order = (5, 7, 3)
    attn_out, top, delta, dq, *parts = run_forward(
        z, scalars, queries, out_grad, start, state, [slot[b] for b in order], order, 3
    )
    part = dict(zip(order, parts, strict=True))
    got = {b: swap(part[b ^ 1], 1) for b in (4, 6, 2)}
    some = (4, 6, 2)
    dq, *parts = run_backward(
        z, scalars, queries, out_grad, start, (top, delta, dq), [slot[b] for b in some], some, False
    )
    part.update(zip(some, parts, strict=True))

    def pair(bit):
        return (part[bit].astype(F32) + got[bit].astype(F32)).astype(BF)

    dq, *ready = lax.optimization_barrier((dq, *(pair(b) for b in some)))
    came = {bit: swap(x, bit) for bit, x in zip(some, ready, strict=True)}
    rest = (1, 0, OWN)
    grad_query, *parts = run_backward(
        z, scalars, queries, out_grad, start, (top, delta, dq), [slot[b] for b in rest], rest, True
    )
    part.update(zip(rest, parts, strict=True))
    mine = part[OWN]
    others = part[0].astype(F32)
    for bits in ((4, 6), (2,)):
        total = sum(came[b].astype(F32) for b in bits)
        behind = (place & bits[0]) == 0
        mine = mine + jnp.where(behind, total, 0.0)
        others = others + jnp.where(behind, 0.0, total)
    last = [give_back(part[1], 1), shift(others.astype(BF), -REACH)]
    mine = mine + sum(x.astype(F32) for x in last)
    return (attn_out, grad_query, mine[:, :width], mine[:, width:])


def solution(mesh):
    rows = P(AXES, None)
    return jax.shard_map(
        on_device,
        mesh=mesh,
        in_specs=(rows, rows, rows, rows, P(), P(AXES)),
        out_specs=(rows, rows, rows, rows),
        check_vma=False,
    )
```

time: 257 us -> 66.2 us (0.26)
  the two profiles are of different devices: /device:TPU:7 before, /device:TPU:1 now
where the time goes in v1:
time: 66.2 us; the launch traced here: 65.2 us
  starting transfers between devices  31.4 us (47%)
  waiting for transfers between devices  19.7 us (30%)
  Pallas kernels  9.88 us (15%)
  local copies, waits for them, and re-layouts  2.4 us (4%)
  between operations  1.47 us (2%)
    ppermute x13, starting transfers between devices, swap(): return lax.ppermute(x, AXES, [(i, i ^ bit) for i in range(devices)])  18 us
    ppermute x13, waiting for transfers between devices, swap(): return lax.ppermute(x, AXES, [(i, i ^ bit) for i in range(devices)])  12.6 us
    ppermute x2, starting transfers between devices, shift(): return lax.ppermute(x, AXES, pairs)  8.74 us
    ppermute x2, waiting for transfers between devices, shift(): return lax.ppermute(x, AXES, pairs)  7.15 us
    pallas_call x3, Pallas kernels, run_forward(): pl.pallas_call(functools.partial(forward_kernel, z, order, not state, ear...  6.53 us
    ppermute x1, starting transfers between devices, give_back(): return lax.ppermute(x, AXES, [(i, j) for i, j in pairs if j >= 0])  4.66 us
    pallas_call x2, Pallas kernels, run_backward(): pl.pallas_call(functools.partial(backward_kernel, z, order, last), out_sh...  2.57 us
    unnamed x10, local copies, waits for them, and re-layouts  1.68 us
  transfers between devices with their start and end apart: 16, of which 8 were waited for; matrix products, arithmetic and copies ran while one was open for 0% of the time, Pallas kernels for 9%

profile of v1, /device:TPU:1, one launch (start us, length us, event | category | flops | bytes accessed | tf_op | source)
XLA Modules:
  0.0 65.2 jit_solution(11110162865697335639)
XLA Ops:
  0.6 0.8 %copy-done = bf16[256,128]{1,0:T(8,128)(2,1)S(1)} copy-done((bf16[256,128]{1,0:T(8,128)(2,1)S(1)}, bf16[256,128]{1,0:T(8,128)(2,1)}, u32[]{:S(2)}) %copy-start) | copy-done | bytes 65560
  1.5 0.8 %copy-done.1 = bf16[256,128]{1,0:T(8,128)(2,1)S(1)} copy-done((bf16[256,128]{1,0:T(8,128)(2,1)S(1)}, bf16[256,128]{1,0:T(8,128)(2,1)}, u32[]{:S(2)}) %copy-start.1) | copy-done | bytes 65560
  2.4 4.6 %collective-permute-start = (bf16[256,256]{1,0:T(8,128)(2,1)S(1)}, bf16[256,256]{1,0:T(8,128)(2,1)S(1)}, u32[]{:S(2)}, u32[]{:S(2)}) collective-permute-start(bf16[256,256]{1,0:T(8,128)(2,1)S(1)} %shard_map.94.refs_6_.kv_ref.refs_11_), channel_id=1, source_target_pairs={{0,8},{1,9},{2,10},{3,11},{4,12},{5,13},{6,14},{7,15},{8,16},{9,17... | collective-permute-start | bytes 393224 | tf_op jit(solution)/shard_map/ppermute | solution.py:351
  7.0 1.9 %collective-permute-done.refs_5_.before_ref.refs_10_ = bf16[256,256]{1,0:T(8,128)(2,1)S(1)} collective-permute-done((bf16[256,256]{1,0:T(8,128)(2,1)S(1)}, bf16[256,256]{1,0:T(8,128)(2,1)S(1)}, u32[]{:S(2)}, u32[]{:S(2)}) %collective-permute-start) | collective-permute-done | bytes 131104 | tf_op jit(solution)/shard_map/ppermute | solution.py:351
  9.0 2.4 %collective-permute-start.1 = (bf16[256,256]{1,0:T(8,128)(2,1)S(1)}, bf16[256,256]{1,0:T(8,128)(2,1)S(1)}, u32[]{:S(2)}, u32[]{:S(2)}) collective-permute-start(bf16[256,256]{1,0:T(8,128)(2,1)S(1)} %get-tuple-element.39), channel_id=1, source_target_pairs={{0,4},{1,5},{2,6},{3,7},{4,0},{5,1},{6,2},{7,3},{8,12},{9,13},{10,... | collective-permute-start | bytes 393224 | tf_op jit(solution)/shard_map/ppermute | solution.py:347
  11.4 1.3 %collective-permute-start.3 = (bf16[256,256]{1,0:T(8,128)(2,1)S(1)}, bf16[256,256]{1,0:T(8,128)(2,1)S(1)}, u32[]{:S(2)}, u32[]{:S(2)}) collective-permute-start(bf16[256,256]{1,0:T(8,128)(2,1)S(1)} %get-tuple-element.40), channel_id=1, source_target_pairs={{0,2},{1,3},{2,0},{3,1},{4,6},{5,7},{6,4},{7,5},{8,10},{9,11},{10,... | collective-permute-start | bytes 393224 | tf_op jit(solution)/shard_map/ppermute | solution.py:347
  12.7 3.2 %collective-permute-done.1.refs_8_.refs_9_ = bf16[256,256]{1,0:T(8,128)(2,1)S(1)} collective-permute-done((bf16[256,256]{1,0:T(8,128)(2,1)S(1)}, bf16[256,256]{1,0:T(8,128)(2,1)S(1)}, u32[]{:S(2)}, u32[]{:S(2)}) %collective-permute-start.1) | collective-permute-done | bytes 131104 | tf_op jit(solution)/shard_map/ppermute | solution.py:347
  15.9 1.6 %collective-permute-start.5 = (bf16[256,256]{1,0:T(8,128)(2,1)S(1)}, bf16[256,256]{1,0:T(8,128)(2,1)S(1)}, u32[]{:S(2)}, u32[]{:S(2)}) collective-permute-start(bf16[256,256]{1,0:T(8,128)(2,1)S(1)} %collective-permute-done.1.refs_8_.refs_9_), channel_id=1, source_target_pairs={{0,1},{1,0},{2,3},{3,2},{4,5},{5,4},{6,7},{7,6},{8,9},{9,8},{10,11... | collective-permute-start | bytes 393224 | tf_op jit(solution)/shard_map/ppermute | solution.py:347
  17.5 0.8 %collective-permute-start.2 = (bf16[256,256]{1,0:T(8,128)(2,1)S(1)}, bf16[256,256]{1,0:T(8,128)(2,1)S(1)}, u32[]{:S(2)}, u32[]{:S(2)}) collective-permute-start(bf16[256,256]{1,0:T(8,128)(2,1)S(1)} %collective-permute-done.1.refs_8_.refs_9_), channel_id=1, source_target_pairs={{0,2},{1,3},{2,0},{3,1},{4,6},{5,7},{6,4},{7,5},{8,10},{9,11},{10,... | collective-permute-start | bytes 393224 | tf_op jit(solution)/shard_map/ppermute | solution.py:347
  19.1 0.7 %shard_map.93 = (s32[1,256]{1,0:T(1,128)S(1)}, s32[1]{0:T(128)}) custom-call(s32[1]{0:T(128)} %bitcast.1.me_ref, s32[64,128]{1,0:T(8,128)S(1)} %bitcast.3), custom_call_target="tpu_custom_call" | custom-call | tf_op jit(solution)/shard_map/pallas_call | solution.py:366
  19.8 1.8 %shard_map.95 = (f32[8,2048]{1,0:T(8,128)S(1)}, f32[8,2048]{1,0:T(8,128)S(1)}, f32[128,2048]{1,0:T(8,128)S(1)}) custom-call(s32[1]{0:T(128)} %bitcast.refs_0_.place_ref, s32[1]{0:T(128)} %get-tuple-element.34.refs_1_, s32[1]{0:T(128)S(6)} %copy.10.refs_2_, bf16[256,1024]{1,0:T(8,128)(2,1)S(1)} %copy-done.3, s32[1,256]{1,0:T(1,128)S(1)} %get-tuple-element.35.refs_4_.refs_5_, ...), custom_call_target="tpu_custom_call" | custom-call | flops 1073741824 | bytes 6291456 | tf_op jit(solution)/shard_map/pallas_call | solution.py:304
  21.6 1.3 %collective-permute-start.7 = (bf16[256,256]{1,0:T(8,128)(2,1)S(1)}, bf16[256,256]{1,0:T(8,128)(2,1)S(1)}, u32[]{:S(2)}, u32[]{:S(2)}) collective-permute-start(bf16[256,256]{1,0:T(8,128)(2,1)S(1)} %collective-permute-done.3.refs_10_.refs_11_), channel_id=1, source_target_pairs={{0,1},{1,0},{2,3},{3,2},{4,5},{5,4},{6,7},{7,6},{8,9},{9,8},{10,11... | collective-permute-start | bytes 393224 | tf_op jit(solution)/shard_map/ppermute | solution.py:347
  22.9 0.8 %collective-permute-start.6 = (bf16[256,256]{1,0:T(8,128)(2,1)S(1)}, bf16[256,256]{1,0:T(8,128)(2,1)S(1)}, u32[]{:S(2)}, u32[]{:S(2)}) collective-permute-start(bf16[256,256]{1,0:T(8,128)(2,1)S(1)} %collective-permute-done.5.refs_9_), channel_id=1, source_target_pairs={{0,2},{1,3},{2,0},{3,1},{4,6},{5,7},{6,4},{7,5},{8,10},{9,11},{10,... | collective-permute-start | bytes 393224 | tf_op jit(solution)/shard_map/ppermute | solution.py:347
  23.7 1.1 %shard_map.97 = (f32[8,2048]{1,0:T(8,128)S(1)}, f32[8,2048]{1,0:T(8,128)S(1)}, f32[128,2048]{1,0:T(8,128)S(1)}) custom-call(s32[1]{0:T(128)} %bitcast.refs_0_.place_ref, s32[1]{0:T(128)} %get-tuple-element.34.refs_1_, s32[1]{0:T(128)S(6)} %copy.10.refs_2_, bf16[256,1024]{1,0:T(8,128)(2,1)S(1)} %copy-done.3, s32[1,256]{1,0:T(1,128)S(1)} %get-tuple-element.35.refs_4_.refs_5_, ...), custom_call_target="tpu_custom_call" | custom-call | flops 2147483648 | bytes 6291456 | tf_op jit(solution)/shard_map/pallas_call | solution.py:304
  24.8 1.3 %collective-permute-done.7.refs_11_ = bf16[256,256]{1,0:T(8,128)(2,1)S(1)} collective-permute-done((bf16[256,256]{1,0:T(8,128)(2,1)S(1)}, bf16[256,256]{1,0:T(8,128)(2,1)S(1)}, u32[]{:S(2)}, u32[]{:S(2)}) %collective-permute-start.7) | collective-permute-done | bytes 131104 | tf_op jit(solution)/shard_map/ppermute | solution.py:347
  26.1 0.9 %collective-permute-done.6.refs_10_ = bf16[256,256]{1,0:T(8,128)(2,1)S(1)} collective-permute-done((bf16[256,256]{1,0:T(8,128)(2,1)S(1)}, bf16[256,256]{1,0:T(8,128)(2,1)S(1)}, u32[]{:S(2)}, u32[]{:S(2)}) %collective-permute-start.6) | collective-permute-done | bytes 131104 | tf_op jit(solution)/shard_map/ppermute | solution.py:347
  27.0 3.6 %shard_map.98 = (bf16[256,1024]{1,0:T(8,128)(2,1)}, f32[8,2048]{1,0:T(8,128)S(1)}, f32[8,2048]{1,0:T(8,128)S(1)}, f32[128,2048]{1,0:T(8,128)S(1)}, bf16[256,256]...) custom-call(s32[1]{0:T(128)} %bitcast.refs_0_.place_ref, s32[1]{0:T(128)} %get-tuple-element.34.refs_1_, ...), custom_call_target="tpu_custom_call" | custom-call | flops 1610612736 | bytes 6291456 | tf_op jit(solution)/shard_map/pallas_call | solution.py:304
  30.7 1.5 %collective-permute-start.9 = (bf16[256,256]{1,0:T(8,128)(2,1)S(1)}, bf16[256,256]{1,0:T(8,128)(2,1)S(1)}, u32[]{:S(2)}, u32[]{:S(2)}) collective-permute-start(bf16[256,256]{1,0:T(8,128)(2,1)S(1)} %get-tuple-element.53), channel_id=1, source_target_pairs={{0,1},{1,0},{2,3},{3,2},{4,5},{5,4},{6,7},{7,6},{8,9},{9,8},{10,11... | collective-permute-start | bytes 393224 | tf_op jit(solution)/shard_map/ppermute | solution.py:347
  32.2 1.0 %shard_map.99 = (f32[128,2048]{1,0:T(8,128)S(1)}, bf16[256,256]{1,0:T(8,128)(2,1)S(1)}, bf16[256,256]{1,0:T(8,128)(2,1)S(1)}, bf16[256,256]{1,0:T(8,128)(2,1)S(1)}) custom-call(s32[1]{0:T(128)} %bitcast.refs_0_.place_ref, s32[1]{0:T(128)} %get-tuple-element.34.refs_1_, s32[1]{0:T(128)S(6)} %copy.10.refs_2_, bf16[256,1024]{1,0:T(8,128)(2,1)S(1)} %copy-done.3, ...), custom_call_target="tpu_custom_call" | custom-call | flops 4026531840 | bytes 6291456 | tf_op jit(solution)/shard_map/pallas_call | solution.py:320
  33.2 1.3 %collective-permute-done.10 = bf16[256,256]{1,0:T(8,128)(2,1)S(1)} collective-permute-done((bf16[256,256]{1,0:T(8,128)(2,1)S(1)}, bf16[256,256]{1,0:T(8,128)(2,1)S(1)}, u32[]{:S(2)}, u32[]{:S(2)}) %collective-permute-start.10) | collective-permute-done | bytes 131104 | tf_op jit(solution)/shard_map/ppermute | solution.py:347
  34.5 3.0 %collective-permute-done.9 = bf16[256,256]{1,0:T(8,128)(2,1)S(1)} collective-permute-done((bf16[256,256]{1,0:T(8,128)(2,1)S(1)}, bf16[256,256]{1,0:T(8,128)(2,1)S(1)}, u32[]{:S(2)}, u32[]{:S(2)}) %collective-permute-start.9) | collective-permute-done | bytes 131104 | tf_op jit(solution)/shard_map/ppermute | solution.py:347
  37.6 2.8 %collective-permute-done.8 = bf16[256,256]{1,0:T(8,128)(2,1)S(1)} collective-permute-done((bf16[256,256]{1,0:T(8,128)(2,1)S(1)}, bf16[256,256]{1,0:T(8,128)(2,1)S(1)}, u32[]{:S(2)}, u32[]{:S(2)}) %collective-permute-start.8) | collective-permute-done | bytes 131104 | tf_op jit(solution)/shard_map/ppermute | solution.py:347
  40.4 1.6 %collective-permute-start.11 = (bf16[256,256]{1,0:T(8,128)(2,1)S(1)}, bf16[256,256]{1,0:T(8,128)(2,1)S(1)}, u32[]{:S(2)}, u32[]{:S(2)}) collective-permute-start(bf16[256,256]{1,0:T(8,128)(2,1)S(1)} %add_convert_fusion.2), channel_id=1, source_target_pairs={{0,4},{1,5},{2,6},{3,7},{4,0},{5,1},{6,2},{7,3},{8,12},{9,13},{10,... | collective-permute-start | bytes 393224 | tf_op jit(solution)/shard_map/ppermute | solution.py:347
  42.0 6.5 %collective-permute-start.12 = (bf16[256,256]{1,0:T(8,128)(2,1)S(1)}, bf16[256,256]{1,0:T(8,128)(2,1)S(1)}, u32[]{:S(2)}, u32[]{:S(2)}) collective-permute-start(bf16[256,256]{1,0:T(8,128)(2,1)S(1)} %add_convert_fusion.1), channel_id=1, source_target_pairs={{0,6},{1,7},{2,4},{3,5},{4,2},{5,3},{6,0},{7,1},{8,14},{9,15},{10,... | collective-permute-start | bytes 393224 | tf_op jit(solution)/shard_map/ppermute | solution.py:347
  48.4 0.2 collective-permute-start.13
  48.6 1.6 %shard_map.100 = (bf16[256,1024]{1,0:T(8,128)(2,1)}, bf16[256,256]{1,0:T(8,128)(2,1)S(1)}, bf16[256,256]{1,0:T(8,128)(2,1)S(1)}, f32[256,256]{1,0:T(8,128)S(1)}) custom-call(s32[1]{0:T(128)} %bitcast.refs_0_.place_ref, s32[1]{0:T(128)} %get-tuple-element.34.refs_1_, s32[1]{0:T(128)S(6)} %copy.10.refs_2_, bf16[256,1024]{1,0:T(8,128)(2,1)S(1)} %copy-done.3, ...), custom_call_target="tpu_custom_call" | custom-call | flops 4026531840 | bytes 6291456 | tf_op jit(solution)/shard_map/pallas_call | solution.py:320
  50.2 4.7 %collective-permute-start.14 = (bf16[256,256]{1,0:T(8,128)(2,1)S(1)}, bf16[256,256]{1,0:T(8,128)(2,1)S(1)}, u32[]{:S(2)}, u32[]{:S(2)}) collective-permute-start(bf16[256,256]{1,0:T(8,128)(2,1)S(1)} %get-tuple-element.62), channel_id=1, source_target_pairs={{1,0},{3,2},{5,4},{7,6},{8,1},{9,8},{10,3},{11,10},{12,5},{13,12},... | collective-permute-start | bytes 393224 | tf_op jit(solution)/shard_map/ppermute | solution.py:355
  54.9 0.1 fusion.3
  55.0 4.1 %collective-permute-start.15 = (bf16[256,256]{1,0:T(8,128)(2,1)S(1)}, bf16[256,256]{1,0:T(8,128)(2,1)S(1)}, u32[]{:S(2)}, u32[]{:S(2)}) collective-permute-start(bf16[256,256]{1,0:T(8,128)(2,1)S(1)} %fusion.3), channel_id=1, source_target_pairs={{8,0},{9,1},{10,2},{11,3},{12,4},{13,5},{14,6},{15,7},{16,8},{17,9... | collective-permute-start | bytes 393224 | tf_op jit(solution)/shard_map/ppermute | solution.py:351
  59.1 5.2 %collective-permute-done.15 = bf16[256,256]{1,0:T(8,128)(2,1)S(1)} collective-permute-done((bf16[256,256]{1,0:T(8,128)(2,1)S(1)}, bf16[256,256]{1,0:T(8,128)(2,1)S(1)}, u32[]{:S(2)}, u32[]{:S(2)}) %collective-permute-start.15) | collective-permute-done | bytes 131104 | tf_op jit(solution)/shard_map/ppermute | solution.py:351
  64.3 0.1 fusion.1
  64.5 0.7 %fusion.4 = (f32[256,128]{1,0:T(8,128)}, f32[256,128]{1,0:T(8,128)}) fusion(f32[256,256]{1,0:T(8,128)S(1)} %fusion.1), kind=kLoop, calls=%fused_computation.10 | loop fusion | bytes 524288 | tf_op jit(solution)/shard_map/slice | solution.py:419
  (24 shorter events, 0.3 us)
Async XLA Ops:
  0.6 0.8 %copy-start = (bf16[256,128]{1,0:T(8,128)(2,1)S(1)}, bf16[256,128]{1,0:T(8,128)(2,1)}, u32[]{:S(2)}) copy-start(bf16[256,128]{1,0:T(8,128)(2,1)} %k_ref.1) | copy-start | bytes 196612
  1.5 0.8 %copy-start.1 = (bf16[256,128]{1,0:T(8,128)(2,1)S(1)}, bf16[256,128]{1,0:T(8,128)(2,1)}, u32[]{:S(2)}) copy-start(bf16[256,128]{1,0:T(8,128)(2,1)} %v_ref.1) | copy-start | bytes 196612
  2.3 17.4 %copy-start.3 = (bf16[256,1024]{1,0:T(8,128)(2,1)S(1)}, bf16[256,1024]{1,0:T(8,128)(2,1)}, u32[]{:S(2)}) copy-start(bf16[256,1024]{1,0:T(8,128)(2,1)} %refs_3_.9) | copy-start | bytes 1572868
  2.4 6.6 %collective-permute-start = (bf16[256,256]{1,0:T(8,128)(2,1)S(1)}, bf16[256,256]{1,0:T(8,128)(2,1)S(1)}, u32[]{:S(2)}, u32[]{:S(2)}) collective-permute-start(bf16[256,256]{1,0:T(8,128)(2,1)S(1)} %shard_map.94.refs_6_.kv_ref.refs_11_), channel_id=1, source_target_pairs={{0,8},{1,9},{2,10},{3,11},{4,12},{5,13},{6,14},{7,15},{8,16},{9,17... | collective-permute-start | bytes 393224 | tf_op jit(solution)/shard_map/ppermute | solution.py:351
  8.9 10.1 %copy-start.2 = (s32[8192]{0:T(1024)S(1)}, s32[8192]{0:T(1024)}, u32[]{:S(2)}) copy-start(s32[8192]{0:T(1024)} %param.10) | copy-start | bytes 98308
  9.0 6.9 %collective-permute-start.1 = (bf16[256,256]{1,0:T(8,128)(2,1)S(1)}, bf16[256,256]{1,0:T(8,128)(2,1)S(1)}, u32[]{:S(2)}, u32[]{:S(2)}) collective-permute-start(bf16[256,256]{1,0:T(8,128)(2,1)S(1)} %get-tuple-element.39), channel_id=1, source_target_pairs={{0,4},{1,5},{2,6},{3,7},{4,0},{5,1},{6,2},{7,3},{8,12},{9,13},{10,... | collective-permute-start | bytes 393224 | tf_op jit(solution)/shard_map/ppermute | solution.py:347
  11.4 10.2 %collective-permute-start.3 = (bf16[256,256]{1,0:T(8,128)(2,1)S(1)}, bf16[256,256]{1,0:T(8,128)(2,1)S(1)}, u32[]{:S(2)}, u32[]{:S(2)}) collective-permute-start(bf16[256,256]{1,0:T(8,128)(2,1)S(1)} %get-tuple-element.40), channel_id=1, source_target_pairs={{0,2},{1,3},{2,0},{3,1},{4,6},{5,7},{6,4},{7,5},{8,10},{9,11},{10,... | collective-permute-start | bytes 393224 | tf_op jit(solution)/shard_map/ppermute | solution.py:347
  15.9 7.0 %collective-permute-start.5 = (bf16[256,256]{1,0:T(8,128)(2,1)S(1)}, bf16[256,256]{1,0:T(8,128)(2,1)S(1)}, u32[]{:S(2)}, u32[]{:S(2)}) collective-permute-start(bf16[256,256]{1,0:T(8,128)(2,1)S(1)} %collective-permute-done.1.refs_8_.refs_9_), channel_id=1, source_target_pairs={{0,1},{1,0},{2,3},{3,2},{4,5},{5,4},{6,7},{7,6},{8,9},{9,8},{10,11... | collective-permute-start | bytes 393224 | tf_op jit(solution)/shard_map/ppermute | solution.py:347
  17.5 6.2 %collective-permute-start.4 = (bf16[256,256]{1,0:T(8,128)(2,1)S(1)}, bf16[256,256]{1,0:T(8,128)(2,1)S(1)}, u32[]{:S(2)}, u32[]{:S(2)}) collective-permute-start(bf16[256,256]{1,0:T(8,128)(2,1)S(1)} %get-tuple-element.41), channel_id=1, source_target_pairs={{0,1},{1,0},{2,3},{3,2},{4,5},{5,4},{6,7},{7,6},{8,9},{9,8},{10,11... | collective-permute-start | bytes 393224 | tf_op jit(solution)/shard_map/ppermute | solution.py:347
  17.5 6.2 %collective-permute-start.2 = (bf16[256,256]{1,0:T(8,128)(2,1)S(1)}, bf16[256,256]{1,0:T(8,128)(2,1)S(1)}, u32[]{:S(2)}, u32[]{:S(2)}) collective-permute-start(bf16[256,256]{1,0:T(8,128)(2,1)S(1)} %collective-permute-done.1.refs_8_.refs_9_), channel_id=1, source_target_pairs={{0,2},{1,3},{2,0},{3,1},{4,6},{5,7},{6,4},{7,5},{8,10},{9,11},{10,... | collective-permute-start | bytes 393224 | tf_op jit(solution)/shard_map/ppermute | solution.py:347
  21.6 4.5 %collective-permute-start.7 = (bf16[256,256]{1,0:T(8,128)(2,1)S(1)}, bf16[256,256]{1,0:T(8,128)(2,1)S(1)}, u32[]{:S(2)}, u32[]{:S(2)}) collective-permute-start(bf16[256,256]{1,0:T(8,128)(2,1)S(1)} %collective-permute-done.3.refs_10_.refs_11_), channel_id=1, source_target_pairs={{0,1},{1,0},{2,3},{3,2},{4,5},{5,4},{6,7},{7,6},{8,9},{9,8},{10,11... | collective-permute-start | bytes 393224 | tf_op jit(solution)/shard_map/ppermute | solution.py:347
  22.9 4.1 %collective-permute-start.6 = (bf16[256,256]{1,0:T(8,128)(2,1)S(1)}, bf16[256,256]{1,0:T(8,128)(2,1)S(1)}, u32[]{:S(2)}, u32[]{:S(2)}) collective-permute-start(bf16[256,256]{1,0:T(8,128)(2,1)S(1)} %collective-permute-done.5.refs_9_), channel_id=1, source_target_pairs={{0,2},{1,3},{2,0},{3,1},{4,6},{5,7},{6,4},{7,5},{8,10},{9,11},{10,... | collective-permute-start | bytes 393224 | tf_op jit(solution)/shard_map/ppermute | solution.py:347
  23.7 3.3 %copy-start.4 = (bf16[256,1024]{1,0:T(8,128)(2,1)S(1)}, bf16[256,1024]{1,0:T(8,128)(2,1)}, u32[]{:S(2)}) copy-start(bf16[256,1024]{1,0:T(8,128)(2,1)} %refs_4_.5) | copy-start | bytes 1572868
  30.7 3.8 %collective-permute-start.10 = (bf16[256,256]{1,0:T(8,128)(2,1)S(1)}, bf16[256,256]{1,0:T(8,128)(2,1)S(1)}, u32[]{:S(2)}, u32[]{:S(2)}) collective-permute-start(bf16[256,256]{1,0:T(8,128)(2,1)S(1)} %get-tuple-element.55), channel_id=1, source_target_pairs={{0,1},{1,0},{2,3},{3,2},{4,5},{5,4},{6,7},{7,6},{8,9},{9,8},{10,11... | collective-permute-start | bytes 393224 | tf_op jit(solution)/shard_map/ppermute | solution.py:347
  30.7 6.9 %collective-permute-start.9 = (bf16[256,256]{1,0:T(8,128)(2,1)S(1)}, bf16[256,256]{1,0:T(8,128)(2,1)S(1)}, u32[]{:S(2)}, u32[]{:S(2)}) collective-permute-start(bf16[256,256]{1,0:T(8,128)(2,1)S(1)} %get-tuple-element.53), channel_id=1, source_target_pairs={{0,1},{1,0},{2,3},{3,2},{4,5},{5,4},{6,7},{7,6},{8,9},{9,8},{10,11... | collective-permute-start | bytes 393224 | tf_op jit(solution)/shard_map/ppermute | solution.py:347
  32.1 8.2 %collective-permute-start.8 = (bf16[256,256]{1,0:T(8,128)(2,1)S(1)}, bf16[256,256]{1,0:T(8,128)(2,1)S(1)}, u32[]{:S(2)}, u32[]{:S(2)}) collective-permute-start(bf16[256,256]{1,0:T(8,128)(2,1)S(1)} %get-tuple-element.51), channel_id=1, source_target_pairs={{0,1},{1,0},{2,3},{3,2},{4,5},{5,4},{6,7},{7,6},{8,9},{9,8},{10,11... | collective-permute-start | bytes 393224 | tf_op jit(solution)/shard_map/ppermute | solution.py:347
  40.4 14.5 %collective-permute-start.11 = (bf16[256,256]{1,0:T(8,128)(2,1)S(1)}, bf16[256,256]{1,0:T(8,128)(2,1)S(1)}, u32[]{:S(2)}, u32[]{:S(2)}) collective-permute-start(bf16[256,256]{1,0:T(8,128)(2,1)S(1)} %add_convert_fusion.2), channel_id=1, source_target_pairs={{0,4},{1,5},{2,6},{3,7},{4,0},{5,1},{6,2},{7,3},{8,12},{9,13},{10,... | collective-permute-start | bytes 393224 | tf_op jit(solution)/shard_map/ppermute | solution.py:347
  42.0 12.9 %collective-permute-start.12 = (bf16[256,256]{1,0:T(8,128)(2,1)S(1)}, bf16[256,256]{1,0:T(8,128)(2,1)S(1)}, u32[]{:S(2)}, u32[]{:S(2)}) collective-permute-start(bf16[256,256]{1,0:T(8,128)(2,1)S(1)} %add_convert_fusion.1), channel_id=1, source_target_pairs={{0,6},{1,7},{2,4},{3,5},{4,2},{5,3},{6,0},{7,1},{8,14},{9,15},{10,... | collective-permute-start | bytes 393224 | tf_op jit(solution)/shard_map/ppermute | solution.py:347
  48.4 6.5 %collective-permute-start.13 = (bf16[256,256]{1,0:T(8,128)(2,1)S(1)}, bf16[256,256]{1,0:T(8,128)(2,1)S(1)}, u32[]{:S(2)}, u32[]{:S(2)}) collective-permute-start(bf16[256,256]{1,0:T(8,128)(2,1)S(1)} %add_convert_fusion), channel_id=1, source_target_pairs={{0,2},{1,3},{2,0},{3,1},{4,6},{5,7},{6,4},{7,5},{8,10},{9,11},{10,... | collective-permute-start | bytes 393224 | tf_op jit(solution)/shard_map/ppermute | solution.py:347
  50.2 8.9 %collective-permute-start.14 = (bf16[256,256]{1,0:T(8,128)(2,1)S(1)}, bf16[256,256]{1,0:T(8,128)(2,1)S(1)}, u32[]{:S(2)}, u32[]{:S(2)}) collective-permute-start(bf16[256,256]{1,0:T(8,128)(2,1)S(1)} %get-tuple-element.62), channel_id=1, source_target_pairs={{1,0},{3,2},{5,4},{7,6},{8,1},{9,8},{10,3},{11,10},{12,5},{13,12},... | collective-permute-start | bytes 393224 | tf_op jit(solution)/shard_map/ppermute | solution.py:355
  55.0 9.4 %collective-permute-start.15 = (bf16[256,256]{1,0:T(8,128)(2,1)S(1)}, bf16[256,256]{1,0:T(8,128)(2,1)S(1)}, u32[]{:S(2)}, u32[]{:S(2)}) collective-permute-start(bf16[256,256]{1,0:T(8,128)(2,1)S(1)} %fusion.3), channel_id=1, source_target_pairs={{8,0},{9,1},{10,2},{11,3},{12,4},{13,5},{14,6},{15,7},{16,8},{17,9... | collective-permute-start | bytes 393224 | tf_op jit(solution)/shard_map/ppermute | solution.py:351
